TPU v7x, 256 devices: a whole 4x4x8 slice. The times are simulated.
256 devices in a mesh: redist: 32 (over z, x_lo, core), summa: 8 (over y, x_hi).
Axes of the slice: x: 4 (x_hi: 2, x_lo: 2; x = x_hi * 2 + x_lo), y: 4, z: 8, core: 2. Of those that a mesh axis runs over, the one named last changes fastest.
Arguments:
- amplitudes: float32 [1024, 22528], P('summa', 'redist'), may hold values from -6 to 6
- integrals: float32 [22528, 22528], P('redist', 'summa'), may hold values from -0.0390625 to 0.0390625
Outputs:
- ladder: float32 [1024, 22528], P('redist', 'summa')
All inputs are finite; a program needn't handle non-finite values.
Results may differ from a plain program's by a relative error of at most 0.000075.
Values sent between devices are 32-bit elements; how exact they have to be, the bound alone decides.
No kernel may reach another device: no remote copies, remote signals or barrier semaphores. Data moves between devices by JAX's collectives and lax.ppermute only.
A program may use at most 64 MiB of HBM per device.

v0:
```python
import jax
import jax.numpy as jnp
from jax import lax
from jax.sharding import PartitionSpec as P


def spread(x, axis, root):
    mine = lax.axis_index(axis) == root
    return lax.psum(jnp.where(mine, x, jnp.zeros_like(x)), axis)


def per_device(amplitudes, integrals):
    local_pairs = amplitudes.shape[0]
    group_size = lax.axis_size("summa")

    def one_root(root_index, running):
        panel_rows = spread(amplitudes, "summa", root_index)
        product = jnp.dot(
            panel_rows,
            integrals,
            precision=lax.Precision.HIGHEST,
            preferred_element_type=jnp.float32,
        )
        return lax.dynamic_update_slice_in_dim(running, product, root_index * local_pairs, 0)

    initial = jnp.zeros((local_pairs * group_size, integrals.shape[1]), jnp.float32)
    partial_sum = lax.fori_loop(0, group_size, one_root, initial)
    products = lax.psum_scatter(partial_sum, "redist", scatter_dimension=0, tiled=True)
    return 0.5 * products


def solution(mesh):
    return jax.shard_map(
        per_device,
        mesh=mesh,
        in_specs=(P("summa", "redist"), P("redist", "summa")),
        out_specs=P("redist", "summa"),
        check_vma=False,
    )
```

profile of v0, /device:TPU:4, one launch (start us, length us, event | category | flops | bytes accessed | tf_op | source)
XLA Modules:
  0.0 968.7 jit_solution(6335014470412838200)
XLA Ops:
  7.4 5.1 broadcast_in_dim.3
  12.5 802.4 %while.13 = (s32[]{:T(128)}, f32[1024,2816]{1,0:T(8,128)}, f32[128,704]{0,1:T(8,128)S(1)}, f32[704,2816]{1,0:T(8,128)}, s32[]{:T(128)}, /*index=5*/s32[]{:T(128)}, s32[]{:T(128)}, s32[]{:T(128)}, u32[]{:T(128)}) while((s32[]{:T(128)}, f32[1024,2816]{1,0:T(8,128)}, f32[128,704]{0,1:T(8,128)S(1)}, f32[704,2816]{1,0:T(8,128)}, s32[]{:T(128)}, ...), condition=%wide.region_2.3_spmd, body=%wide.region_0.2_spmd.sunk | while | flops 3045244928 | bytes 12615901 | solution.py:27
  12.5 0.8 broadcast_select_fusion.2
  13.2 0.0 all-reduce.2.cloned.1.call-update
  13.3 92.1 %all-reduce.2.cloned.1.call-done = f32[128,704]{0,1:T(8,128)} async-done(((f32[128,704]{0,1:T(8,128)}), f32[128,704]{0,1:T(8,128)}) %all-reduce.2.cloned.1.call-update) | async-done | bytes 360464 | tf_op jit(solution)/shard_map/while/body/eval_jaxpr/psum | solution.py:9
  105.3 8.7 convolution_dynamic-update-slice_fusion.2
  114.0 0.8 broadcast_select_fusion.2
  114.8 0.0 all-reduce.2.cloned.1.call-update
  114.8 90.8 %all-reduce.2.cloned.1.call-done = f32[128,704]{0,1:T(8,128)} async-done(((f32[128,704]{0,1:T(8,128)}), f32[128,704]{0,1:T(8,128)}) %all-reduce.2.cloned.1.call-update) | async-done | bytes 360464 | tf_op jit(solution)/shard_map/while/body/eval_jaxpr/psum | solution.py:9
  205.6 8.6 convolution_dynamic-update-slice_fusion.2
  214.2 0.8 broadcast_select_fusion.2
  215.0 0.0 all-reduce.2.cloned.1.call-update
  215.0 90.8 %all-reduce.2.cloned.1.call-done = f32[128,704]{0,1:T(8,128)} async-done(((f32[128,704]{0,1:T(8,128)}), f32[128,704]{0,1:T(8,128)}) %all-reduce.2.cloned.1.call-update) | async-done | bytes 360464 | tf_op jit(solution)/shard_map/while/body/eval_jaxpr/psum | solution.py:9
  305.8 8.7 convolution_dynamic-update-slice_fusion.2
  314.5 0.8 broadcast_select_fusion.2
  315.3 90.5 %all-reduce.2.cloned.1.call-done = f32[128,704]{0,1:T(8,128)} async-done(((f32[128,704]{0,1:T(8,128)}), f32[128,704]{0,1:T(8,128)}) %all-reduce.2.cloned.1.call-update) | async-done | bytes 360464 | tf_op jit(solution)/shard_map/while/body/eval_jaxpr/psum | solution.py:9
  405.7 8.7 convolution_dynamic-update-slice_fusion.2
  414.4 0.8 broadcast_select_fusion.2
  415.2 90.5 %all-reduce.2.cloned.1.call-done = f32[128,704]{0,1:T(8,128)} async-done(((f32[128,704]{0,1:T(8,128)}), f32[128,704]{0,1:T(8,128)}) %all-reduce.2.cloned.1.call-update) | async-done | bytes 360464 | tf_op jit(solution)/shard_map/while/body/eval_jaxpr/psum | solution.py:9
  505.7 8.7 convolution_dynamic-update-slice_fusion.2
  514.4 0.8 broadcast_select_fusion.2
  515.1 90.5 %all-reduce.2.cloned.1.call-done = f32[128,704]{0,1:T(8,128)} async-done(((f32[128,704]{0,1:T(8,128)}), f32[128,704]{0,1:T(8,128)}) %all-reduce.2.cloned.1.call-update) | async-done | bytes 360464 | tf_op jit(solution)/shard_map/while/body/eval_jaxpr/psum | solution.py:9
  605.6 8.7 convolution_dynamic-update-slice_fusion.2
  614.3 0.8 broadcast_select_fusion.2
  615.1 90.8 %all-reduce.2.cloned.1.call-done = f32[128,704]{0,1:T(8,128)} async-done(((f32[128,704]{0,1:T(8,128)}), f32[128,704]{0,1:T(8,128)}) %all-reduce.2.cloned.1.call-update) | async-done | bytes 360464 | tf_op jit(solution)/shard_map/while/body/eval_jaxpr/psum | solution.py:9
  705.9 8.7 convolution_dynamic-update-slice_fusion.2
  714.6 0.8 broadcast_select_fusion.2
  715.4 90.8 %all-reduce.2.cloned.1.call-done = f32[128,704]{0,1:T(8,128)} async-done(((f32[128,704]{0,1:T(8,128)}), f32[128,704]{0,1:T(8,128)}) %all-reduce.2.cloned.1.call-update) | async-done | bytes 360464 | tf_op jit(solution)/shard_map/while/body/eval_jaxpr/psum | solution.py:9
  806.2 8.6 convolution_dynamic-update-slice_fusion.2
  814.8 0.6 reduce-scatter.2.cloned.1.call-update
  815.4 144.2 %reduce-scatter.2.cloned.1.call-done = f32[32,2816]{1,0:T(8,128)} async-done(((f32[1024,2816]{1,0:T(8,128)}), f32[32,2816]{1,0:T(8,128)}) %reduce-scatter.2.cloned.1.call-update) | async-done | bytes 360464 | tf_op jit(solution)/shard_map/reduce_scatter | solution.py:28
  959.5 1.7 broadcast_multiply_fusion
  (16 shorter events, 0.1 us)
Async XLA Ops:
  7.4 5.1 copy-start
  12.5 92.9 %all-reduce.2.cloned.1.call-start = ((), (), s32[]{:S(2)}) async-start(), calls=%async_computation.2 | async-start | bytes 720896 | tf_op jit(solution)/shard_map/while/body/eval_jaxpr/psum | solution.py:9
  114.0 91.6 %all-reduce.2.cloned.1.call-start = ((), (), s32[]{:S(2)}) async-start(), calls=%async_computation.2 | async-start | bytes 720896 | tf_op jit(solution)/shard_map/while/body/eval_jaxpr/psum | solution.py:9
  214.2 91.6 %all-reduce.2.cloned.1.call-start = ((), (), s32[]{:S(2)}) async-start(), calls=%async_computation.2 | async-start | bytes 720896 | tf_op jit(solution)/shard_map/while/body/eval_jaxpr/psum | solution.py:9
  314.5 91.3 %all-reduce.2.cloned.1.call-start = ((), (), s32[]{:S(2)}) async-start(), calls=%async_computation.2 | async-start | bytes 720896 | tf_op jit(solution)/shard_map/while/body/eval_jaxpr/psum | solution.py:9
  414.4 91.3 %all-reduce.2.cloned.1.call-start = ((), (), s32[]{:S(2)}) async-start(), calls=%async_computation.2 | async-start | bytes 720896 | tf_op jit(solution)/shard_map/while/body/eval_jaxpr/psum | solution.py:9
  514.3 91.3 %all-reduce.2.cloned.1.call-start = ((), (), s32[]{:S(2)}) async-start(), calls=%async_computation.2 | async-start | bytes 720896 | tf_op jit(solution)/shard_map/while/body/eval_jaxpr/psum | solution.py:9
  614.3 91.6 %all-reduce.2.cloned.1.call-start = ((), (), s32[]{:S(2)}) async-start(), calls=%async_computation.2 | async-start | bytes 720896 | tf_op jit(solution)/shard_map/while/body/eval_jaxpr/psum | solution.py:9
  714.6 91.6 %all-reduce.2.cloned.1.call-start = ((), (), s32[]{:S(2)}) async-start(), calls=%async_computation.2 | async-start | bytes 720896 | tf_op jit(solution)/shard_map/while/body/eval_jaxpr/psum | solution.py:9
  814.8 144.7 %reduce-scatter.2.cloned.1.call-start = ((), (), s32[]{:S(2)}) async-start(), calls=%async_computation.1 | async-start | bytes 11894784 | tf_op jit(solution)/shard_map/reduce_scatter | solution.py:28
Sparse Core Ops, SparseCore 0:
  15.9 89.3 all-reduce.1
  117.5 88.0 all-reduce.1
  217.7 88.0 all-reduce.1
  317.6 88.0 all-reduce.1
  417.6 88.0 all-reduce.1
  517.5 88.0 all-reduce.1
  617.8 88.0 all-reduce.1
  718.1 88.0 all-reduce.1
Sparse Core Ops, SparseCore 1:
  817.8 141.6 reduce-scatter.1
where the time goes:
time: 971 us; the launch traced here: 969 us
  waiting for transfers between devices  871 us (90%)
  matrix products  69.3 us (7%)
  between operations  14.8 us (2%)
    psum x8, waiting for transfers between devices, spread(): return lax.psum(jnp.where(mine, x, jnp.zeros_like(x)), axis)  727 us
    reduce_scatter x1, waiting for transfers between devices, per_device(): lax.psum_scatter(partial_sum, 'redist', scatter_dimension=0, tiled=True)  144 us
    dot_general x8, matrix products, one_root(): jnp.dot(panel_rows, integrals, precision=lax.Precision.HIGHEST, preferred...  69.3 us
  transfers between devices with their start and end apart: 9, of which 9 were waited for; matrix products, arithmetic and copies ran while one was open for 0% of the time, Pallas kernels for 0%

commit v1 on v0

v1 whole, which is shorter than its diff:
```python
import functools

import jax
import jax.numpy as jnp
from jax import lax
from jax.experimental import pallas as pl
from jax.experimental.pallas import tpu as pltpu
from jax.sharding import Mesh, PartitionSpec as P

X_FIRST = 10
TILE = 256

SLOTS = 0x63745210

VMEM = pl.BlockSpec(memory_space=pltpu.VMEM)
SMEM = pl.BlockSpec(memory_space=pltpu.SMEM)
ANY = pl.BlockSpec(memory_space=pl.ANY)
HBM = pl.BlockSpec(memory_space=pltpu.HBM)

HEAVY, LIGHT = 20_000_000_000, 1


def shift(x, axis, by):
    n = lax.axis_size(axis)
    return lax.ppermute(x, axis, [(i, (i + by) % n) for i in range(n)])


def local(body, ins, deps, outs, scratch=(), scalars=(), through=(), pinned=True, big=(), weight=HEAVY):
    pin = lambda x: pltpu.with_memory_space_constraint(x, pltpu.VMEM)
    sizes = [len(scalars), len(ins), len(big), len(through), len(deps), len(outs), len(through), len(scratch)]

    def kernel(*refs):
        groups, at = [], 0
        for n in sizes:
            groups.append(refs[at : at + n])
            at += n
        s, i, g, _, _, o, _, t = groups
        body(*([s[0]] if s else []), [*i, *g], o, *([t] if t else []))

    kind = pltpu.VMEM if pinned else jax.ShapeDtypeStruct
    first = len(scalars) + len(ins) + len(big)
    return pl.pallas_call(
        kernel,
        in_specs=[SMEM] * len(scalars) + [VMEM] * len(ins) + [HBM] * len(big) + [VMEM] * len(through) + [ANY] * len(deps),
        out_specs=[VMEM] * (len(outs) + len(through)),
        out_shape=[kind(s, d) for s, d in outs] + [pltpu.VMEM(x.shape, x.dtype) for x in through],
        input_output_aliases={first + i: len(outs) + i for i in range(len(through))},
        scratch_shapes=list(scratch),
        compiler_params=pltpu.CompilerParams(vmem_limit_bytes=8 * 1024 * 1024),
        cost_estimate=pl.CostEstimate(flops=weight, bytes_accessed=1, transcendentals=0),
    )(*scalars, *map(pin, ins), *(pltpu.with_memory_space_constraint(x, pltpu.HBM) for x in big), *map(pin, through), *deps)


def split(x):
    high = x.astype(jnp.bfloat16)
    return high, (x - high.astype(jnp.float32)).astype(jnp.bfloat16)


def rows_in(row_refs, places, a_high, a_low):
    for ref, row, half, slot in places:
        to = half * 256 + slot * 64
        a_high[to : to + 64], a_low[to : to + 64] = split(row_refs[ref][row : row + 64])


def multiply(a_high, a_low, high, low, keep_ref, send_ref, cols):
    mul = functools.partial(jnp.dot, preferred_element_type=jnp.float32)
    sums = mul(a_high[...], high) + (mul(a_low[...], high) + mul(a_high[...], low))
    keep_ref[:, cols] = sums[:256]
    send_ref[:, cols] = sums[256:]


def tile(i):
    return pl.ds(pl.multiple_of(i * TILE, TILE), TILE)


def early_products(panels, places, b, first, tiles, deps, through=(), weight=HEAVY):
    depth = b.shape[0]

    def body(ins, outs, scratch):
        *row_refs, b_ref = ins
        keep_ref, send_ref, high_ref, low_ref = outs
        a_high, a_low, held, sems = scratch

        def fetch(i):
            return pltpu.make_async_copy(b_ref.at[:, tile(first + i)], held.at[i & 1], sems.at[i & 1])

        fetch(0).start()
        rows_in(row_refs, places, a_high, a_low)

        @pl.loop(0, tiles)
        def _(i):
            @pl.when(i + 1 < tiles)
            def _():
                fetch(i + 1).start()

            fetch(i).wait()
            high, low = split(held[i & 1])
            high_ref[:, tile(i)], low_ref[:, tile(i)] = high, low
            multiply(a_high, a_low, high, low, keep_ref, send_ref, tile(i))

    width = tiles * TILE
    outs = [((256, width), jnp.float32)] * 2 + [((depth, width), jnp.bfloat16)] * 2
    scratch = [pltpu.VMEM((512, depth), jnp.bfloat16)] * 2
    scratch += [pltpu.VMEM((2, depth, TILE), jnp.float32), pltpu.SemaphoreType.DMA((2,))]
    return local(body, panels, deps, outs, scratch, through=through, big=[b], weight=weight)


def late_products(panels, places, high, low, deps):
    depth, width = high.shape

    def body(ins, outs, scratch):
        *row_refs, high_ref, low_ref = ins
        a_high, a_low = scratch
        rows_in(row_refs, places, a_high, a_low)

        @pl.loop(0, width // TILE)
        def _(i):
            multiply(a_high, a_low, high_ref[:, tile(i)], low_ref[:, tile(i)], *outs, tile(i))

    outs = [((256, width), jnp.float32)] * 2
    return local(body, [*panels, high, low], deps, outs, [pltpu.VMEM((512, depth), jnp.bfloat16)] * 2)


def late_halves(up, down, deps):
    def body(ins, outs):
        outs[0][...] = ins[0][:64]
        outs[1][...] = ins[1][64:128]

    return local(body, [up, down], deps, [((64, up.shape[1]), jnp.float32)] * 2)


def x_part(kept, got, deps):
    def body(ins, outs):
        for i in range(4):
            rows = slice(64 * i + 32, 64 * i + 64)
            outs[0][32 * i : 32 * i + 32] = ins[0][rows] + ins[1][rows]

    return local(body, [kept, got], deps, [((128, kept.shape[1]), jnp.float32)])[0]


class Ring:
    def __init__(self, slots, lots, n):
        self.slots, self.lots, self.n = slots, lots, n
        self.i = 4
        self.width = lots[0][0].shape[1]

    def kernel(self, ins, moves, outs, deps):
        n, count, sources = self.n, len(ins), [*self.lots[0], *self.lots[1]]
        strides = [v.shape[0] // 4 for v in self.lots[0]]

        def body(slots, refs, out_refs):
            lots = refs[count : count + len(strides)], refs[count + len(strides) :]
            for out, at, k, low, adds in moves:
                s = slots[k % 8]

                def write(lot, s):
                    total = sum(
                        ref[pl.ds(pl.multiple_of(s * stride + low, n), n)] for ref, stride in zip(lot, strides)
                    )
                    for source, row in adds:
                        total = total + refs[source][row : row + n]
                    out_refs[out][at : at + n] = total

                pl.when(s < 4)(functools.partial(write, lots[0], s))
                pl.when(s >= 4)(functools.partial(write, lots[1], s - 4))

        shapes = [((rows, self.width), jnp.float32) for rows in outs]
        return local(body, [*ins, *sources], deps, shapes, scalars=[self.slots])

    def begin(self, deps):
        n = self.n
        moves = [(0, 0, 4, 0, ()), (0, n, 3, n, ()), (1, 0, -4, n, ()), (1, n, -3, 0, ())]
        self.sends = self.kernel([], moves, [2 * n, 2 * n], deps)

    def hop(self):
        self.got = [shift(self.sends[0], "z", 1), shift(self.sends[1], "z", -1)]

    def add(self, deps):
        n = self.n
        self.i -= 1
        i = self.i
        if i > 1:
            moves = [
                (0, 0, i, 0, [(0, 0)]),
                (0, n, i - 1, n, [(0, n)]),
                (1, 0, -i, n, [(1, 0)]),
                (1, n, 1 - i, 0, [(1, n)]),
            ]
            self.sends = self.kernel(self.got, moves, [2 * n, 2 * n], deps)
        elif i == 1:
            self.rest = self.got
            moves = [(0, 0, 1, 0, [(0, 0)]), (1, 0, -1, n, [(1, 0)])]
            self.sends = self.kernel(self.got, moves, [n, n], deps)
        else:
            moves = [(0, 0, 0, 0, [(0, 0), (3, n)]), (1, 0, 0, n, [(1, 0), (2, n)])]
            return self.kernel([*self.got, *self.rest], moves, [n, n], deps)


def finish(left, from_x, right_a, right_b):
    cut = left.shape[1]

    def body(ins, outs):
        out = outs[0]
        out[:, :cut] = 0.5 * (ins[0][...] + ins[1][...])
        out[:16, cut:] = 0.5 * ins[2][...]
        out[16:, cut:] = 0.5 * ins[3][...]

    shape = (32, cut + right_a.shape[1])
    return local(body, [left, from_x, right_a, right_b], [], [(shape, jnp.float32)], pinned=False)[0]


def per_device(amplitudes, integrals):
    z, xl, c = (lax.axis_index(n) for n in ("z", "xl", "c"))
    y, xh = lax.axis_index("y"), lax.axis_index("xh")
    depth, width = integrals.shape
    x_tiles = X_FIRST * 128 // TILE
    z_tiles = width // TILE - x_tiles

    owner = (z + jnp.arange(8, dtype=jnp.int32)) & 7
    code = (((owner >> 1) - y) & 3) * 2 + ((owner ^ xh) & 1)
    slots = (SLOTS >> (code * 4)) & 7

    own = amplitudes.reshape(2, 2, 32, depth)
    own = jnp.where(xl == 1, own[::-1], own)
    own = jnp.where(c == 1, own[:, ::-1], own)
    own = own.transpose(1, 0, 2, 3).reshape(128, depth)

    up, down, other = shift(own, "y", 1), shift(own, "y", -1), shift(own, "xh", 1)
    up2 = shift(jnp.concatenate([other, up[:64]], 0), "y", 1)
    down2 = shift(jnp.concatenate([other, down[64:]], 0), "y", -1)

    early = [own, other, down, up]
    early_places = [(i, 64 * half, half, i) for i in range(4) for half in range(2)]
    late_places = [(0, 128, 0, 0), (1, 128, 1, 0), (2, 0, 0, 3), (3, 0, 1, 3)]
    late_places += [(ref, 64 * half, half, slot) for slot, ref in ((1, 1), (2, 0)) for half in range(2)]

    kept_x0, sent_x0, *b_x = early_products(early, early_places, integrals, z_tiles, x_tiles, [])
    kept_z0, sent_z0, *b_z, sent_x0 = early_products(
        early, early_places, integrals, 0, z_tiles, [kept_x0], [sent_x0], LIGHT
    )
    got_x0, got_z0 = shift(sent_x0, "c", 1), shift(sent_z0, "c", 1)
    far_up, far_down = late_halves(up2, down2, [kept_z0])
    late = [up2, down2, shift(far_up, "y", 1), shift(far_down, "y", -1)]
    x_send0 = x_part(kept_x0, got_x0, [far_up])
    other0 = shift(x_send0, "xl", 1)

    kept_z1, sent_z1 = late_products(late, late_places, *b_z, [x_send0])
    got_z1 = shift(sent_z1, "c", 1)
    kept_x1, sent_x1 = late_products(late, late_places, *b_x, [kept_z1])
    got_x1 = shift(sent_x1, "c", 1)

    first = Ring(slots, ([kept_z0, got_z0], [kept_z1, got_z1]), 32)
    first.begin([kept_x1])
    first.hop()
    x_send1 = x_part(kept_x1, got_x1, [*first.sends, other0])
    other1 = shift(x_send1, "xl", 1)
    first.add([x_send1])
    first.hop()
    second = Ring(slots, ([kept_x0, got_x0, other0], [kept_x1, got_x1, other1]), 16)
    second.begin(first.sends)
    for _ in range(2):
        second.hop()
        first.add(second.sends)
        first.hop()
        second.add(first.sends)
    second.hop()
    near, far_sum = first.add(second.sends)
    from_x = shift(far_sum, "xl", 1)
    second.add([far_sum])
    second.hop()
    right = second.add([])
    return finish(near, from_x, *right)


def solution(mesh):
    fine = Mesh(mesh.devices.reshape(8, 2, 2, 4, 2), ("z", "xl", "c", "y", "xh"))
    redist, summa = ("z", "xl", "c"), ("y", "xh")
    return jax.shard_map(
        per_device,
        mesh=fine,
        in_specs=(P(summa, redist), P(redist, summa)),
        out_specs=P(redist, summa),
        check_vma=False,
    )
```

time: 971 us -> 119 us (0.12)
  waiting for transfers between devices: 871 us -> 43.5 us
  matrix products: 69.3 us -> 0 us
  starting transfers between devices: 0.02 us -> 44.2 us
  Pallas kernels: 0 us -> 29 us
  between operations: 14.8 us -> 0.22 us
    psum x8 -> x0, waiting for transfers between devices: 727 us -> none  [spread(): return lax.psum(jnp.where(mine, x, jnp.zeros_like(x)), axis)]
    reduce_scatter x1 -> x0, waiting for transfers between devices: 144 us -> none  [per_device(): lax.psum_scatter(partial_sum, 'redist', scatter_dimension=0, tiled=True)]
    dot_general x8 -> x0, matrix products: 69.3 us -> none  [one_root(): jnp.dot(panel_rows, integrals, precision=lax.Precision.HIGHEST, preferred...]
    ppermute x0 -> x30, starting transfers between devices: none -> 44.2 us  [shift(): return lax.ppermute(x, axis, [(i, (i + by) % n) for i in range(n)])]
    ppermute x0 -> x30, waiting for transfers between devices: none -> 43.5 us  [shift(): return lax.ppermute(x, axis, [(i, (i + by) % n) for i in range(n)])]
    pallas_call x0 -> x18, Pallas kernels: none -> 29 us  [local(): pl.pallas_call(kernel, in_specs=[SMEM] * len(scalars) + [VMEM] * len(ins)...]
  transfers between devices with their start and end apart: 9 -> 30, of which waited for: 9 -> 15; matrix products, arithmetic and copies ran while one was open for 0% -> 0% of each run, Pallas kernels for 0% -> 23%
where the time goes in v1:
time: 119 us; the launch traced here: 118 us
  starting transfers between devices  44.2 us (37%)
  waiting for transfers between devices  43.5 us (37%)
  Pallas kernels  29 us (24%)
  local copies, waits for them, and re-layouts  1.2 us (1%)
    ppermute x30, starting transfers between devices, shift(): return lax.ppermute(x, axis, [(i, (i + by) % n) for i in range(n)])  44.2 us
    ppermute x30, waiting for transfers between devices, shift(): return lax.ppermute(x, axis, [(i, (i + by) % n) for i in range(n)])  43.5 us
    pallas_call x18, Pallas kernels, local(): pl.pallas_call(kernel, in_specs=[SMEM] * len(scalars) + [VMEM] * len(ins)...  29 us
  transfers between devices with their start and end apart: 30, of which 15 were waited for; matrix products, arithmetic and copies ran while one was open for 0% of the time, Pallas kernels for 23%

profile of v1, /device:TPU:4, one launch (start us, length us, event | category | flops | bytes accessed | tf_op | source)
XLA Modules:
  0.0 118.2 jit_solution(9071754133142906788)
XLA Ops:
  1.3 1.7 %collective-permute-start.2 = (f32[128,704]{1,0:T(8,128)S(1)}, f32[128,704]{1,0:T(8,128)S(1)}, u32[]{:S(2)}, u32[]{:S(2)}) collective-permute-start(f32[128,704]{1,0:T(8,128)S(1)} %bitcast.4), channel_id=1, source_target_pairs={{0,2},{2,4},{4,6},{6,0},{1,3},{3,5},{5,7},{7,1},{8,10},{10,12},{12... | collective-permute-start | bytes 1081352 | tf_op jit(solution)/shard_map/ppermute | solution.py:25
  2.9 1.7 %collective-permute-start.1 = (f32[128,704]{1,0:T(8,128)S(1)}, f32[128,704]{1,0:T(8,128)S(1)}, u32[]{:S(2)}, u32[]{:S(2)}) collective-permute-start(f32[128,704]{1,0:T(8,128)S(1)} %bitcast.5), channel_id=1, source_target_pairs={{0,6},{2,0},{4,2},{6,4},{1,7},{3,1},{5,3},{7,5},{8,14},{10,8},{12,... | collective-permute-start | bytes 1081352 | tf_op jit(solution)/shard_map/ppermute | solution.py:25
  4.6 2.2 %collective-permute-start = (f32[128,704]{1,0:T(8,128)S(1)}, f32[128,704]{1,0:T(8,128)S(1)}, u32[]{:S(2)}, u32[]{:S(2)}) collective-permute-start(f32[128,704]{1,0:T(8,128)S(1)} %bitcast.6), channel_id=1, source_target_pairs={{0,1},{1,0},{2,3},{3,2},{4,5},{5,4},{6,7},{7,6},{8,9},{9,8},{10,11... | collective-permute-start | bytes 1081352 | tf_op jit(solution)/shard_map/ppermute | solution.py:25
  6.8 6.6 %collective-permute-done.2.refs_3_ = f32[128,704]{1,0:T(8,128)S(1)} collective-permute-done((f32[128,704]{1,0:T(8,128)S(1)}, f32[128,704]{1,0:T(8,128)S(1)}, u32[]{:S(2)}, u32[]{:S(2)}) %collective-permute-start.2) | collective-permute-done | bytes 360480 | tf_op jit(solution)/shard_map/ppermute | solution.py:25
  13.5 3.0 %collective-permute-done.refs_1_ = f32[128,704]{1,0:T(8,128)S(1)} collective-permute-done((f32[128,704]{1,0:T(8,128)S(1)}, f32[128,704]{1,0:T(8,128)S(1)}, u32[]{:S(2)}, u32[]{:S(2)}) %collective-permute-start) | collective-permute-done | bytes 360480 | tf_op jit(solution)/shard_map/ppermute | solution.py:25
  16.6 1.7 %collective-permute-start.5 = (f32[192,704]{1,0:T(8,128)S(1)}, f32[192,704]{1,0:T(8,128)S(1)}, u32[]{:S(2)}, u32[]{:S(2)}) collective-permute-start(f32[192,704]{1,0:T(8,128)S(1)} %get-tuple-element.75), channel_id=1, source_target_pairs={{0,6},{2,0},{4,2},{6,4},{1,7},{3,1},{5,3},{7,5},{8,14},{10,8},{12,... | collective-permute-start | bytes 1622024 | tf_op jit(solution)/shard_map/ppermute | solution.py:25
  18.7 5.8 %shard_map.28 = (f32[256,1280]{1,0:T(8,128)S(1)}, f32[256,1280]{1,0:T(8,128)S(1)}, bf16[704,1280]{1,0:T(8,128)(2,1)S(1)}, bf16[704,1280]{1,0:T(8,128)(2,1)S(1)}) custom-call(f32[128,704]{1,0:T(8,128)S(1)} %bitcast.7, f32[128,704]{1,0:T(8,128)S(1)} %collective-permute-done.refs_1_, f32[128,704]{1,0:T(8,128)S(1)} %collective-permute-done.1.refs_2_, ...), custom_call_target="tpu_custom_call" | custom-call | flops 20000000000 | bytes 1 | tf_op jit(solution)/shard_map/pallas_call | solution.py:42
  24.5 6.7 %shard_map.29 = (f32[256,1536]{1,0:T(8,128)S(1)}, f32[256,1536]{1,0:T(8,128)S(1)}, bf16[704,1536]{1,0:T(8,128)(2,1)S(1)}, bf16[704,1536]{1,0:T(8,128)(2,1)S(1)}, f32[256,1280]{1,0:T(8,128)S(1)}) custom-call(f32[128,704]{1,0:T(8,128)S(1)} %bitcast.8, f32[128,704]{1,0:T(8,128)S(1)} %collective-permute-done.refs_1_, ...), custom_call_target="tpu_custom_call", output_to_operand_aliasing={{4}: (5, {})} | custom-call | flops 1 | bytes 1 | tf_op jit(solution)/shard_map/pallas_call | solution.py:42
  32.9 1.9 %collective-permute-start.7 = (f32[64,704]{1,0:T(8,128)S(1)}, f32[64,704]{1,0:T(8,128)S(1)}, u32[]{:S(2)}, u32[]{:S(2)}) collective-permute-start(f32[64,704]{1,0:T(8,128)S(1)} %get-tuple-element.45), channel_id=1, source_target_pairs={{0,6},{2,0},{4,2},{6,4},{1,7},{3,1},{5,3},{7,5},{8,14},{10,8},{12,... | collective-permute-start | bytes 540680 | tf_op jit(solution)/shard_map/ppermute | solution.py:25
  35.1 1.3 %collective-permute-start.13 = (f32[128,1280]{1,0:T(8,128)S(1)}, f32[128,1280]{1,0:T(8,128)S(1)}, u32[]{:S(2)}, u32[]{:S(2)}) collective-permute-start(f32[128,1280]{1,0:T(8,128)S(1)} %shard_map.31.refs_6_), channel_id=1, source_target_pairs={{0,16},{16,0},{1,17},{17,1},{2,18},{18,2},{3,19},{19,3},{4,20},{20... | collective-permute-start | bytes 1966088 | tf_op jit(solution)/shard_map/ppermute | solution.py:25
  36.4 2.9 %collective-permute-done.7.refs_3_ = f32[64,704]{1,0:T(8,128)S(1)} collective-permute-done((f32[64,704]{1,0:T(8,128)S(1)}, f32[64,704]{1,0:T(8,128)S(1)}, u32[]{:S(2)}, u32[]{:S(2)}) %collective-permute-start.7) | collective-permute-done | bytes 180256 | tf_op jit(solution)/shard_map/ppermute | solution.py:25
  39.2 3.4 %collective-permute-done.6.refs_2_ = f32[64,704]{1,0:T(8,128)S(1)} collective-permute-done((f32[64,704]{1,0:T(8,128)S(1)}, f32[64,704]{1,0:T(8,128)S(1)}, u32[]{:S(2)}, u32[]{:S(2)}) %collective-permute-start.6) | collective-permute-done | bytes 180256 | tf_op jit(solution)/shard_map/ppermute | solution.py:25
  42.7 4.9 %shard_map.32 = (f32[256,1536]{1,0:T(8,128)S(1)}, f32[256,1536]{1,0:T(8,128)S(1)}) custom-call(f32[192,704]{1,0:T(8,128)S(1)} %collective-permute-done.4.refs_0_, f32[192,704]{1,0:T(8,128)S(1)} %collective-permute-done.5.refs_1_, f32[64,704]{1,0:T(8,128)S(1)} %collective-permute-done.6.refs_2_, f32[64,704]{1,0:T(8,128)S(1)} %collective-permute-done.7.refs_3_, ...), custom_call_target="tpu_custom_call" | custom-call | flops 20000000000 | bytes 1 | tf_op jit(solution)/shard_map/pallas_call | solution.py:42
  47.7 4.1 %shard_map.33 = (f32[256,1280]{1,0:T(8,128)S(1)}, f32[256,1280]{1,0:T(8,128)S(1)}) custom-call(f32[192,704]{1,0:T(8,128)S(1)} %collective-permute-done.4.refs_0_, f32[192,704]{1,0:T(8,128)S(1)} %collective-permute-done.5.refs_1_, f32[64,704]{1,0:T(8,128)S(1)} %collective-permute-done.6.refs_2_, f32[64,704]{1,0:T(8,128)S(1)} %collective-permute-done.7.refs_3_, ...), custom_call_target="tpu_custom_call" | custom-call | flops 20000000000 | bytes 1 | tf_op jit(solution)/shard_map/pallas_call | solution.py:42
  53.1 2.2 %collective-permute-start.10 = (f32[64,1536]{1,0:T(8,128)S(1)}, f32[64,1536]{1,0:T(8,128)S(1)}, u32[]{:S(2)}, u32[]{:S(2)}) collective-permute-start(f32[64,1536]{1,0:T(8,128)S(1)} %get-tuple-element.54.refs_2_), channel_id=1, source_target_pairs={{0,32},{32,64},{64,96},{96,128},{128,160},{160,192},{192,224},{224... | collective-permute-start | bytes 1179656 | tf_op jit(solution)/shard_map/ppermute | solution.py:25
  55.2 4.0 %collective-permute-start.11 = (f32[64,1536]{1,0:T(8,128)S(1)}, f32[64,1536]{1,0:T(8,128)S(1)}, u32[]{:S(2)}, u32[]{:S(2)}) collective-permute-start(f32[64,1536]{1,0:T(8,128)S(1)} %get-tuple-element.55.refs_3_), channel_id=1, source_target_pairs={{0,224},{32,0},{64,32},{96,64},{128,96},{160,128},{192,160},{224,1... | collective-permute-start | bytes 1179656 | tf_op jit(solution)/shard_map/ppermute | solution.py:25
  59.4 1.3 %collective-permute-start.16 = (f32[128,1280]{1,0:T(8,128)S(1)}, f32[128,1280]{1,0:T(8,128)S(1)}, u32[]{:S(2)}, u32[]{:S(2)}) collective-permute-start(f32[128,1280]{1,0:T(8,128)S(1)} %shard_map.35.refs_7_), channel_id=1, source_target_pairs={{0,16},{16,0},{1,17},{17,1},{2,18},{18,2},{3,19},{19,3},{4,20},{20... | collective-permute-start | bytes 1966088 | tf_op jit(solution)/shard_map/ppermute | solution.py:25
  60.6 7.8 %collective-permute-done.10.refs_1_ = f32[64,1536]{1,0:T(8,128)S(1)} collective-permute-done((f32[64,1536]{1,0:T(8,128)S(1)}, f32[64,1536]{1,0:T(8,128)S(1)}, u32[]{:S(2)}, u32[]{:S(2)}) %collective-permute-start.10) | collective-permute-done | bytes 393248 | tf_op jit(solution)/shard_map/ppermute | solution.py:25
  69.3 3.2 %collective-permute-start.15 = (f32[64,1536]{1,0:T(8,128)S(1)}, f32[64,1536]{1,0:T(8,128)S(1)}, u32[]{:S(2)}, u32[]{:S(2)}) collective-permute-start(f32[64,1536]{1,0:T(8,128)S(1)} %get-tuple-element.58.refs_8_), channel_id=1, source_target_pairs={{0,224},{32,0},{64,32},{96,64},{128,96},{160,128},{192,160},{224,1... | collective-permute-start | bytes 1179656 | tf_op jit(solution)/shard_map/ppermute | solution.py:25
  72.5 3.3 %collective-permute-done.16.refs_6_.refs_8_.refs_10_ = f32[128,1280]{1,0:T(8,128)S(1)} collective-permute-done((f32[128,1280]{1,0:T(8,128)S(1)}, f32[128,1280]{1,0:T(8,128)S(1)}, u32[]{:S(2)}, u32[]{:S(2)}) %collective-permute-start.16) | collective-permute-done | bytes 655392 | tf_op jit(solution)/shard_map/ppermute | solution.py:25
  76.6 3.2 %collective-permute-start.20 = (f32[32,1280]{1,0:T(8,128)S(1)}, f32[32,1280]{1,0:T(8,128)S(1)}, u32[]{:S(2)}, u32[]{:S(2)}) collective-permute-start(f32[32,1280]{1,0:T(8,128)S(1)} %get-tuple-element.60.refs_8_), channel_id=1, source_target_pairs={{0,224},{32,0},{64,32},{96,64},{128,96},{160,128},{192,160},{224,1... | collective-permute-start | bytes 491528 | tf_op jit(solution)/shard_map/ppermute | solution.py:25
  79.8 2.7 %collective-permute-done.14.refs_1_ = f32[64,1536]{1,0:T(8,128)S(1)} collective-permute-done((f32[64,1536]{1,0:T(8,128)S(1)}, f32[64,1536]{1,0:T(8,128)S(1)}, u32[]{:S(2)}, u32[]{:S(2)}) %collective-permute-start.14) | collective-permute-done | bytes 393248 | tf_op jit(solution)/shard_map/ppermute | solution.py:25
  83.3 2.1 %collective-permute-start.17 = (f32[64,1536]{1,0:T(8,128)S(1)}, f32[64,1536]{1,0:T(8,128)S(1)}, u32[]{:S(2)}, u32[]{:S(2)}) collective-permute-start(f32[64,1536]{1,0:T(8,128)S(1)} %get-tuple-element.61.refs_9_), channel_id=1, source_target_pairs={{0,32},{32,64},{64,96},{96,128},{128,160},{160,192},{192,224},{224... | collective-permute-start | bytes 1179656 | tf_op jit(solution)/shard_map/ppermute | solution.py:25
  88.2 2.4 %collective-permute-start.24 = (f32[32,1280]{1,0:T(8,128)S(1)}, f32[32,1280]{1,0:T(8,128)S(1)}, u32[]{:S(2)}, u32[]{:S(2)}) collective-permute-start(f32[32,1280]{1,0:T(8,128)S(1)} %get-tuple-element.64.refs_8_), channel_id=1, source_target_pairs={{0,224},{32,0},{64,32},{96,64},{128,96},{160,128},{192,160},{224,1... | collective-permute-start | bytes 491528 | tf_op jit(solution)/shard_map/ppermute | solution.py:25
  90.6 4.9 %collective-permute-done.17.refs_1_.refs_3_ = f32[64,1536]{1,0:T(8,128)S(1)} collective-permute-done((f32[64,1536]{1,0:T(8,128)S(1)}, f32[64,1536]{1,0:T(8,128)S(1)}, u32[]{:S(2)}, u32[]{:S(2)}) %collective-permute-start.17) | collective-permute-done | bytes 393248 | tf_op jit(solution)/shard_map/ppermute | solution.py:25
  96.0 2.1 %collective-permute-start.21 = (f32[32,1536]{1,0:T(8,128)S(1)}, f32[32,1536]{1,0:T(8,128)S(1)}, u32[]{:S(2)}, u32[]{:S(2)}) collective-permute-start(f32[32,1536]{1,0:T(8,128)S(1)} %get-tuple-element.65.refs_9_), channel_id=1, source_target_pairs={{0,32},{32,64},{64,96},{96,128},{128,160},{160,192},{192,224},{224... | collective-permute-start | bytes 589832 | tf_op jit(solution)/shard_map/ppermute | solution.py:25
  100.0 1.7 %collective-permute-start.26 = (f32[32,1280]{1,0:T(8,128)S(1)}, f32[32,1280]{1,0:T(8,128)S(1)}, u32[]{:S(2)}, u32[]{:S(2)}) collective-permute-start(f32[32,1280]{1,0:T(8,128)S(1)} %get-tuple-element.67.refs_9_), channel_id=1, source_target_pairs={{0,32},{32,64},{64,96},{96,128},{128,160},{160,192},{192,224},{224... | collective-permute-start | bytes 491528 | tf_op jit(solution)/shard_map/ppermute | solution.py:25
  101.7 1.7 %collective-permute-start.27 = (f32[32,1280]{1,0:T(8,128)S(1)}, f32[32,1280]{1,0:T(8,128)S(1)}, u32[]{:S(2)}, u32[]{:S(2)}) collective-permute-start(f32[32,1280]{1,0:T(8,128)S(1)} %get-tuple-element.68.refs_10_), channel_id=1, source_target_pairs={{0,224},{32,0},{64,32},{96,64},{128,96},{160,128},{192,160},{224,1... | collective-permute-start | bytes 491528 | tf_op jit(solution)/shard_map/ppermute | solution.py:25
  104.5 2.8 %collective-permute-done.26.refs_1_.refs_3_ = f32[32,1280]{1,0:T(8,128)S(1)} collective-permute-done((f32[32,1280]{1,0:T(8,128)S(1)}, f32[32,1280]{1,0:T(8,128)S(1)}, u32[]{:S(2)}, u32[]{:S(2)}) %collective-permute-start.26) | collective-permute-done | bytes 163872 | tf_op jit(solution)/shard_map/ppermute | solution.py:25
  108.5 1.8 %collective-permute-start.28 = (f32[16,1280]{1,0:T(8,128)S(1)}, f32[16,1280]{1,0:T(8,128)S(1)}, u32[]{:S(2)}, u32[]{:S(2)}) collective-permute-start(f32[16,1280]{1,0:T(8,128)S(1)} %get-tuple-element.71), channel_id=1, source_target_pairs={{0,32},{32,64},{64,96},{96,128},{128,160},{160,192},{192,224},{224... | collective-permute-start | bytes 245768 | tf_op jit(solution)/shard_map/ppermute | solution.py:25
  110.3 1.5 %collective-permute-start.29 = (f32[16,1280]{1,0:T(8,128)S(1)}, f32[16,1280]{1,0:T(8,128)S(1)}, u32[]{:S(2)}, u32[]{:S(2)}) collective-permute-start(f32[16,1280]{1,0:T(8,128)S(1)} %get-tuple-element.72), channel_id=1, source_target_pairs={{0,224},{32,0},{64,32},{96,64},{128,96},{160,128},{192,160},{224,1... | collective-permute-start | bytes 245768 | tf_op jit(solution)/shard_map/ppermute | solution.py:25
  115.4 2.1 %collective-permute-done.25.refs_1_ = f32[32,1536]{1,0:T(8,128)S(1)} collective-permute-done((f32[32,1536]{1,0:T(8,128)S(1)}, f32[32,1536]{1,0:T(8,128)S(1)}, u32[]{:S(2)}, u32[]{:S(2)}) %collective-permute-start.25) | collective-permute-done | bytes 196640 | tf_op jit(solution)/shard_map/ppermute | solution.py:25
  (54 shorter events, 19.2 us)
Async XLA Ops:
  1.3 12.2 %collective-permute-start.2 = (f32[128,704]{1,0:T(8,128)S(1)}, f32[128,704]{1,0:T(8,128)S(1)}, u32[]{:S(2)}, u32[]{:S(2)}) collective-permute-start(f32[128,704]{1,0:T(8,128)S(1)} %bitcast.4), channel_id=1, source_target_pairs={{0,2},{2,4},{4,6},{6,0},{1,3},{3,5},{5,7},{7,1},{8,10},{10,12},{12... | collective-permute-start | bytes 1081352 | tf_op jit(solution)/shard_map/ppermute | solution.py:25
  2.9 10.6 %collective-permute-start.1 = (f32[128,704]{1,0:T(8,128)S(1)}, f32[128,704]{1,0:T(8,128)S(1)}, u32[]{:S(2)}, u32[]{:S(2)}) collective-permute-start(f32[128,704]{1,0:T(8,128)S(1)} %bitcast.5), channel_id=1, source_target_pairs={{0,6},{2,0},{4,2},{6,4},{1,7},{3,1},{5,3},{7,5},{8,14},{10,8},{12,... | collective-permute-start | bytes 1081352 | tf_op jit(solution)/shard_map/ppermute | solution.py:25
  4.6 11.9 %collective-permute-start = (f32[128,704]{1,0:T(8,128)S(1)}, f32[128,704]{1,0:T(8,128)S(1)}, u32[]{:S(2)}, u32[]{:S(2)}) collective-permute-start(f32[128,704]{1,0:T(8,128)S(1)} %bitcast.6), channel_id=1, source_target_pairs={{0,1},{1,0},{2,3},{3,2},{4,5},{5,4},{6,7},{7,6},{8,9},{9,8},{10,11... | collective-permute-start | bytes 1081352 | tf_op jit(solution)/shard_map/ppermute | solution.py:25
  16.6 15.2 %collective-permute-start.5 = (f32[192,704]{1,0:T(8,128)S(1)}, f32[192,704]{1,0:T(8,128)S(1)}, u32[]{:S(2)}, u32[]{:S(2)}) collective-permute-start(f32[192,704]{1,0:T(8,128)S(1)} %get-tuple-element.75), channel_id=1, source_target_pairs={{0,6},{2,0},{4,2},{6,4},{1,7},{3,1},{5,3},{7,5},{8,14},{10,8},{12,... | collective-permute-start | bytes 1622024 | tf_op jit(solution)/shard_map/ppermute | solution.py:25
  18.3 14.5 %collective-permute-start.4 = (f32[192,704]{1,0:T(8,128)S(1)}, f32[192,704]{1,0:T(8,128)S(1)}, u32[]{:S(2)}, u32[]{:S(2)}) collective-permute-start(f32[192,704]{1,0:T(8,128)S(1)} %get-tuple-element.76), channel_id=1, source_target_pairs={{0,2},{2,4},{4,6},{6,0},{1,3},{3,5},{5,7},{7,1},{8,10},{10,12},{12... | collective-permute-start | bytes 1622024 | tf_op jit(solution)/shard_map/ppermute | solution.py:25
  31.2 3.8 %collective-permute-start.8 = (f32[256,1280]{1,0:T(8,128)S(1)}, f32[256,1280]{1,0:T(8,128)S(1)}, u32[]{:S(2)}, u32[]{:S(2)}) collective-permute-start(f32[256,1280]{1,0:T(8,128)S(1)} %get-tuple-element.48), channel_id=1, source_target_pairs={{0,8},{8,0},{1,9},{9,1},{2,10},{10,2},{3,11},{11,3},{4,12},{12,4},... | collective-permute-start | bytes 3932168 | tf_op jit(solution)/shard_map/ppermute | solution.py:25
  31.3 21.1 %collective-permute-start.3 = (f32[256,1536]{1,0:T(8,128)S(1)}, f32[256,1536]{1,0:T(8,128)S(1)}, u32[]{:S(2)}, u32[]{:S(2)}) collective-permute-start(f32[256,1536]{1,0:T(8,128)S(1)} %get-tuple-element.43), channel_id=1, source_target_pairs={{0,8},{8,0},{1,9},{9,1},{2,10},{10,2},{3,11},{11,3},{4,12},{12,4},... | collective-permute-start | bytes 4718600 | tf_op jit(solution)/shard_map/ppermute | solution.py:25
  32.9 6.4 %collective-permute-start.7 = (f32[64,704]{1,0:T(8,128)S(1)}, f32[64,704]{1,0:T(8,128)S(1)}, u32[]{:S(2)}, u32[]{:S(2)}) collective-permute-start(f32[64,704]{1,0:T(8,128)S(1)} %get-tuple-element.45), channel_id=1, source_target_pairs={{0,6},{2,0},{4,2},{6,4},{1,7},{3,1},{5,3},{7,5},{8,14},{10,8},{12,... | collective-permute-start | bytes 540680 | tf_op jit(solution)/shard_map/ppermute | solution.py:25
  34.8 7.8 %collective-permute-start.6 = (f32[64,704]{1,0:T(8,128)S(1)}, f32[64,704]{1,0:T(8,128)S(1)}, u32[]{:S(2)}, u32[]{:S(2)}) collective-permute-start(f32[64,704]{1,0:T(8,128)S(1)} %get-tuple-element.44.refs_2_), channel_id=1, source_target_pairs={{0,2},{2,4},{4,6},{6,0},{1,3},{3,5},{5,7},{7,1},{8,10},{10,12},{12... | collective-permute-start | bytes 540680 | tf_op jit(solution)/shard_map/ppermute | solution.py:25
  35.1 24.2 %collective-permute-start.13 = (f32[128,1280]{1,0:T(8,128)S(1)}, f32[128,1280]{1,0:T(8,128)S(1)}, u32[]{:S(2)}, u32[]{:S(2)}) collective-permute-start(f32[128,1280]{1,0:T(8,128)S(1)} %shard_map.31.refs_6_), channel_id=1, source_target_pairs={{0,16},{16,0},{1,17},{17,1},{2,18},{18,2},{3,19},{19,3},{4,20},{20... | collective-permute-start | bytes 1966088 | tf_op jit(solution)/shard_map/ppermute | solution.py:25
  47.6 4.8 %collective-permute-start.9 = (f32[256,1536]{1,0:T(8,128)S(1)}, f32[256,1536]{1,0:T(8,128)S(1)}, u32[]{:S(2)}, u32[]{:S(2)}) collective-permute-start(f32[256,1536]{1,0:T(8,128)S(1)} %get-tuple-element.50), channel_id=1, source_target_pairs={{0,8},{8,0},{1,9},{9,1},{2,10},{10,2},{3,11},{11,3},{4,12},{12,4},... | collective-permute-start | bytes 4718600 | tf_op jit(solution)/shard_map/ppermute | solution.py:25
  51.8 7.5 %collective-permute-start.12 = (f32[256,1280]{1,0:T(8,128)S(1)}, f32[256,1280]{1,0:T(8,128)S(1)}, u32[]{:S(2)}, u32[]{:S(2)}) collective-permute-start(f32[256,1280]{1,0:T(8,128)S(1)} %get-tuple-element.56), channel_id=1, source_target_pairs={{0,8},{8,0},{1,9},{9,1},{2,10},{10,2},{3,11},{11,3},{4,12},{12,4},... | collective-permute-start | bytes 3932168 | tf_op jit(solution)/shard_map/ppermute | solution.py:25
  53.1 15.4 %collective-permute-start.10 = (f32[64,1536]{1,0:T(8,128)S(1)}, f32[64,1536]{1,0:T(8,128)S(1)}, u32[]{:S(2)}, u32[]{:S(2)}) collective-permute-start(f32[64,1536]{1,0:T(8,128)S(1)} %get-tuple-element.54.refs_2_), channel_id=1, source_target_pairs={{0,32},{32,64},{64,96},{96,128},{128,160},{160,192},{192,224},{224... | collective-permute-start | bytes 1179656 | tf_op jit(solution)/shard_map/ppermute | solution.py:25
  55.2 13.2 %collective-permute-start.11 = (f32[64,1536]{1,0:T(8,128)S(1)}, f32[64,1536]{1,0:T(8,128)S(1)}, u32[]{:S(2)}, u32[]{:S(2)}) collective-permute-start(f32[64,1536]{1,0:T(8,128)S(1)} %get-tuple-element.55.refs_3_), channel_id=1, source_target_pairs={{0,224},{32,0},{64,32},{96,64},{128,96},{160,128},{192,160},{224,1... | collective-permute-start | bytes 1179656 | tf_op jit(solution)/shard_map/ppermute | solution.py:25
  59.4 16.5 %collective-permute-start.16 = (f32[128,1280]{1,0:T(8,128)S(1)}, f32[128,1280]{1,0:T(8,128)S(1)}, u32[]{:S(2)}, u32[]{:S(2)}) collective-permute-start(f32[128,1280]{1,0:T(8,128)S(1)} %shard_map.35.refs_7_), channel_id=1, source_target_pairs={{0,16},{16,0},{1,17},{17,1},{2,18},{18,2},{3,19},{19,3},{4,20},{20... | collective-permute-start | bytes 1966088 | tf_op jit(solution)/shard_map/ppermute | solution.py:25
  69.2 13.3 %collective-permute-start.14 = (f32[64,1536]{1,0:T(8,128)S(1)}, f32[64,1536]{1,0:T(8,128)S(1)}, u32[]{:S(2)}, u32[]{:S(2)}) collective-permute-start(f32[64,1536]{1,0:T(8,128)S(1)} %get-tuple-element.57.refs_7_), channel_id=1, source_target_pairs={{0,32},{32,64},{64,96},{96,128},{128,160},{160,192},{192,224},{224... | collective-permute-start | bytes 1179656 | tf_op jit(solution)/shard_map/ppermute | solution.py:25
  69.3 13.3 %collective-permute-start.15 = (f32[64,1536]{1,0:T(8,128)S(1)}, f32[64,1536]{1,0:T(8,128)S(1)}, u32[]{:S(2)}, u32[]{:S(2)}) collective-permute-start(f32[64,1536]{1,0:T(8,128)S(1)} %get-tuple-element.58.refs_8_), channel_id=1, source_target_pairs={{0,224},{32,0},{64,32},{96,64},{128,96},{160,128},{192,160},{224,1... | collective-permute-start | bytes 1179656 | tf_op jit(solution)/shard_map/ppermute | solution.py:25
  76.5 10.1 %collective-permute-start.19 = (f32[32,1280]{1,0:T(8,128)S(1)}, f32[32,1280]{1,0:T(8,128)S(1)}, u32[]{:S(2)}, u32[]{:S(2)}) collective-permute-start(f32[32,1280]{1,0:T(8,128)S(1)} %get-tuple-element.59.refs_7_), channel_id=1, source_target_pairs={{0,32},{32,64},{64,96},{96,128},{128,160},{160,192},{192,224},{224... | collective-permute-start | bytes 491528 | tf_op jit(solution)/shard_map/ppermute | solution.py:25
  76.6 10.0 %collective-permute-start.20 = (f32[32,1280]{1,0:T(8,128)S(1)}, f32[32,1280]{1,0:T(8,128)S(1)}, u32[]{:S(2)}, u32[]{:S(2)}) collective-permute-start(f32[32,1280]{1,0:T(8,128)S(1)} %get-tuple-element.60.refs_8_), channel_id=1, source_target_pairs={{0,224},{32,0},{64,32},{96,64},{128,96},{160,128},{192,160},{224,1... | collective-permute-start | bytes 491528 | tf_op jit(solution)/shard_map/ppermute | solution.py:25
  83.3 12.2 %collective-permute-start.17 = (f32[64,1536]{1,0:T(8,128)S(1)}, f32[64,1536]{1,0:T(8,128)S(1)}, u32[]{:S(2)}, u32[]{:S(2)}) collective-permute-start(f32[64,1536]{1,0:T(8,128)S(1)} %get-tuple-element.61.refs_9_), channel_id=1, source_target_pairs={{0,32},{32,64},{64,96},{96,128},{128,160},{160,192},{192,224},{224... | collective-permute-start | bytes 1179656 | tf_op jit(solution)/shard_map/ppermute | solution.py:25
  85.4 10.0 %collective-permute-start.18 = (f32[64,1536]{1,0:T(8,128)S(1)}, f32[64,1536]{1,0:T(8,128)S(1)}, u32[]{:S(2)}, u32[]{:S(2)}) collective-permute-start(f32[64,1536]{1,0:T(8,128)S(1)} %get-tuple-element.62.refs_10_), channel_id=1, source_target_pairs={{0,224},{32,0},{64,32},{96,64},{128,96},{160,128},{192,160},{224,1... | collective-permute-start | bytes 1179656 | tf_op jit(solution)/shard_map/ppermute | solution.py:25
  87.2 12.1 %collective-permute-start.23 = (f32[32,1280]{1,0:T(8,128)S(1)}, f32[32,1280]{1,0:T(8,128)S(1)}, u32[]{:S(2)}, u32[]{:S(2)}) collective-permute-start(f32[32,1280]{1,0:T(8,128)S(1)} %get-tuple-element.63.refs_7_), channel_id=1, source_target_pairs={{0,32},{32,64},{64,96},{96,128},{128,160},{160,192},{192,224},{224... | collective-permute-start | bytes 491528 | tf_op jit(solution)/shard_map/ppermute | solution.py:25
  88.2 11.2 %collective-permute-start.24 = (f32[32,1280]{1,0:T(8,128)S(1)}, f32[32,1280]{1,0:T(8,128)S(1)}, u32[]{:S(2)}, u32[]{:S(2)}) collective-permute-start(f32[32,1280]{1,0:T(8,128)S(1)} %get-tuple-element.64.refs_8_), channel_id=1, source_target_pairs={{0,224},{32,0},{64,32},{96,64},{128,96},{160,128},{192,160},{224,1... | collective-permute-start | bytes 491528 | tf_op jit(solution)/shard_map/ppermute | solution.py:25
  96.0 7.3 %collective-permute-start.21 = (f32[32,1536]{1,0:T(8,128)S(1)}, f32[32,1536]{1,0:T(8,128)S(1)}, u32[]{:S(2)}, u32[]{:S(2)}) collective-permute-start(f32[32,1536]{1,0:T(8,128)S(1)} %get-tuple-element.65.refs_9_), channel_id=1, source_target_pairs={{0,32},{32,64},{64,96},{96,128},{128,160},{160,192},{192,224},{224... | collective-permute-start | bytes 589832 | tf_op jit(solution)/shard_map/ppermute | solution.py:25
  98.2 5.7 %collective-permute-start.22 = (f32[32,1536]{1,0:T(8,128)S(1)}, f32[32,1536]{1,0:T(8,128)S(1)}, u32[]{:S(2)}, u32[]{:S(2)}) collective-permute-start(f32[32,1536]{1,0:T(8,128)S(1)} %get-tuple-element.66.refs_10_), channel_id=1, source_target_pairs={{0,224},{32,0},{64,32},{96,64},{128,96},{160,128},{192,160},{224,1... | collective-permute-start | bytes 589832 | tf_op jit(solution)/shard_map/ppermute | solution.py:25
  100.0 7.2 %collective-permute-start.26 = (f32[32,1280]{1,0:T(8,128)S(1)}, f32[32,1280]{1,0:T(8,128)S(1)}, u32[]{:S(2)}, u32[]{:S(2)}) collective-permute-start(f32[32,1280]{1,0:T(8,128)S(1)} %get-tuple-element.67.refs_9_), channel_id=1, source_target_pairs={{0,32},{32,64},{64,96},{96,128},{128,160},{160,192},{192,224},{224... | collective-permute-start | bytes 491528 | tf_op jit(solution)/shard_map/ppermute | solution.py:25
  101.7 6.2 %collective-permute-start.27 = (f32[32,1280]{1,0:T(8,128)S(1)}, f32[32,1280]{1,0:T(8,128)S(1)}, u32[]{:S(2)}, u32[]{:S(2)}) collective-permute-start(f32[32,1280]{1,0:T(8,128)S(1)} %get-tuple-element.68.refs_10_), channel_id=1, source_target_pairs={{0,224},{32,0},{64,32},{96,64},{128,96},{160,128},{192,160},{224,1... | collective-permute-start | bytes 491528 | tf_op jit(solution)/shard_map/ppermute | solution.py:25
  108.5 5.7 %collective-permute-start.28 = (f32[16,1280]{1,0:T(8,128)S(1)}, f32[16,1280]{1,0:T(8,128)S(1)}, u32[]{:S(2)}, u32[]{:S(2)}) collective-permute-start(f32[16,1280]{1,0:T(8,128)S(1)} %get-tuple-element.71), channel_id=1, source_target_pairs={{0,32},{32,64},{64,96},{96,128},{128,160},{160,192},{192,224},{224... | collective-permute-start | bytes 245768 | tf_op jit(solution)/shard_map/ppermute | solution.py:25
  110.3 4.4 %collective-permute-start.29 = (f32[16,1280]{1,0:T(8,128)S(1)}, f32[16,1280]{1,0:T(8,128)S(1)}, u32[]{:S(2)}, u32[]{:S(2)}) collective-permute-start(f32[16,1280]{1,0:T(8,128)S(1)} %get-tuple-element.72), channel_id=1, source_target_pairs={{0,224},{32,0},{64,32},{96,64},{128,96},{160,128},{192,160},{224,1... | collective-permute-start | bytes 245768 | tf_op jit(solution)/shard_map/ppermute | solution.py:25
  111.8 5.7 %collective-permute-start.25 = (f32[32,1536]{1,0:T(8,128)S(1)}, f32[32,1536]{1,0:T(8,128)S(1)}, u32[]{:S(2)}, u32[]{:S(2)}) collective-permute-start(f32[32,1536]{1,0:T(8,128)S(1)} %get-tuple-element.70.refs_9_), channel_id=1, source_target_pairs={{0,16},{16,0},{1,17},{17,1},{2,18},{18,2},{3,19},{19,3},{4,20},{20... | collective-permute-start | bytes 589832 | tf_op jit(solution)/shard_map/ppermute | solution.py:25
